TPU v7x, 128 devices: a whole 4x4x4 slice. The times are simulated.
128 devices in a mesh: dom: 16 (over x, z_hi, core), sub: 8 (over z_lo, y).
Axes of the slice: x: 4, y: 4, z: 4 (z_hi: 2, z_lo: 2; z = z_hi * 2 + z_lo), core: 2. Of those that a mesh axis runs over, the one named last changes fastest.
Arguments:
- features: float32 [262144, 128], P(('dom', 'sub')), may hold values from -6 to 6
- send_rows: int32 [128, 128, 8], P(('dom', 'sub')), may hold values from 0 to 2047
- hub_rows: int32 [128, 32], P(('dom', 'sub')), may hold values from 0 to 2047
- tile_weights: float32 [2048, 16, 128, 128], P(('dom', 'sub'))
- tile_cols: int32 [2048, 16], P(('dom', 'sub')), may hold values from 0 to 55, as said below
- tile_count: int32 [2048], P(('dom', 'sub')), may hold values from 1 to 16, as said below
- in_degree: int32 [262144], P(('dom', 'sub')), may hold values from 0 to 2048, as said below
- w_self: float32 [128, 128], replicated, may hold values from -0.5 to 0.5
- w_neigh: float32 [128, 128], replicated, may hold values from -0.5 to 0.5
- bias: float32 [128], replicated, may hold values from -3 to 3
Outputs:
- output: float32 [262144, 128], P(('dom', 'sub'))
Inputs may be any that keep to these rules, and one draw needn't show every extreme that they name: `send_rows`: row indices into the sending device's own 2048 rows. `hub_rows`: row indices into the owning device's own 2048 rows. `tile_cols`: indices of 128-row blocks of the receiving device's sources. `tile_count`: some row tile holds 16 used slots in every draw; counts differ widely between devices. `in_degree`: the number of nonzero weights in the node's row over the used slots of its row tile; some node reaches 2048 in every draw.
All inputs are finite; a program needn't handle non-finite values.
Results may differ from a plain program's by a relative error of at most 0.0003.
Values sent between devices are 32-bit elements; how exact they have to be, the bound alone decides.
A program may use at most 128 MiB of HBM per device.

v0:
```python
import jax
import jax.numpy as jnp
from jax import lax
from jax.sharding import PartitionSpec as P


def boundary_exchange(outgoing, feature_width):
    received = lax.all_to_all(outgoing, ("dom", "sub"), split_axis=0, concat_axis=0, tiled=True)
    return received.reshape(-1, feature_width)


def body(
    features,
    send_rows,
    hub_rows,
    tile_weights,
    tile_cols,
    tile_count,
    in_degree,
    w_self,
    w_neigh,
    bias,
):
    feature_width = features.shape[1]
    tile_size = tile_weights.shape[2]
    slot_total = tile_weights.shape[1]
    outgoing = features[send_rows[0]]
    own_hubs = features[hub_rows[0]]
    boundary = boundary_exchange(outgoing, feature_width)
    hub_table = lax.all_gather(own_hubs, ("dom", "sub"), axis=0, tiled=True)
    sources = jnp.concatenate([features, boundary, hub_table], axis=0).reshape(
        -1, tile_size, feature_width
    )
    slot_live = (jnp.arange(slot_total)[None, :] < tile_count[:, None]).astype(jnp.float32)
    blocks = sources[tile_cols]
    summed_tiles = jnp.einsum(
        "rtij,rtjh,rt->rih", tile_weights, blocks, slot_live, precision=lax.Precision.HIGHEST
    )
    summed = summed_tiles.reshape(-1, feature_width)
    degree = jnp.maximum(in_degree, 1).astype(jnp.float32)
    neighbour_mean = summed / degree[:, None]
    hidden = (
        jnp.dot(features, w_self, precision=lax.Precision.HIGHEST)
        + jnp.dot(neighbour_mean, w_neigh, precision=lax.Precision.HIGHEST)
        + bias
    )
    hidden = jax.nn.relu(hidden)
    return hidden * lax.rsqrt(jnp.mean(hidden * hidden, axis=-1, keepdims=True) + 1e-05)


def solution(mesh):
    in_specs = (
        P(("dom", "sub"), None),
        P(("dom", "sub"), None, None),
        P(("dom", "sub"), None),
        P(("dom", "sub"), None, None, None),
        P(("dom", "sub"), None),
        P(("dom", "sub")),
        P(("dom", "sub")),
        P(),
        P(),
        P(),
    )
    out_specs = P(("dom", "sub"), None)
    return jax.shard_map(body, mesh=mesh, in_specs=in_specs, out_specs=out_specs, check_vma=False)
```

profile of v0, /device:TPU:1, one launch (start us, length us, event | category | flops | bytes accessed | tf_op | source)
XLA Modules:
  0.0 363.6 jit_solution(14746793749873843325)
XLA Ops:
  6.5 0.0 copy-start
  6.5 0.0 all-gather.3.cloned.1.call-start
  6.5 0.7 fusion.6
  7.2 2.4 gather_fusion.1
  9.6 0.0 all-gather.3.cloned.1.call-update
  9.6 0.7 compare_select_fusion.1
  10.3 0.1 copy.12
  10.4 0.1 reshape.81
  10.5 5.3 %gather_fusion = f32[1024,128]{1,0:T(8,128)} fusion(f32[2048,128]{1,0:T(8,128)} %param.10, s32[1024]{0:T(1024)S(1)} %broadcast_clamp_fusion), kind=kCustom, calls=%fused_computation | custom fusion | bytes 1052672 | tf_op jit(solution)/shard_map/gather | solution.py:27
  15.8 11.5 %all-to-all-start = ((f32[128,8,128]{2,1,0:T(8,128)}), f32[128,8,128]{2,1,0:T(8,128)S(1)}, u32[]{:S(2)}, u32[]{:S(2)}) async-start(f32[128,8,128]{2,1,0:T(8,128)} %bitcast.1), calls=%async_computation | async-start | bytes 1048576 | tf_op jit(solution)/shard_map/all_to_all | solution.py:8
  27.3 0.7 compare_select_fusion
  28.0 0.1 reshape.97
  28.1 0.7 fusion.5
  28.8 0.7 maximum_convert_fusion
  29.5 2.3 fusion.7
  31.8 9.7 %all-to-all-done = f32[128,8,128]{2,1,0:T(8,128)S(1)} async-done(((f32[128,8,128]{2,1,0:T(8,128)}), f32[128,8,128]{2,1,0:T(8,128)S(1)}, u32[]{:S(2)}, u32[]{:S(2)}) %all-to-all-start) | async-done | bytes 524320 | tf_op jit(solution)/shard_map/all_to_all | solution.py:8
  41.5 273.1 %all-gather.3.cloned.1.call-done = f32[4096,128]{1,0:T(8,128)} async-done(((f32[32,128]{1,0:T(8,128)}), f32[4096,128]{1,0:T(8,128)}) %all-gather.3.cloned.1.call-update) | async-done | bytes 2097168 | tf_op jit(solution)/shard_map/all_gather | solution.py:30
  314.7 3.9 %pad_maximum_fusion = f32[7168,128]{1,0:T(8,128)} fusion(f32[4096,128]{1,0:T(8,128)} %all-gather.3.cloned.1.call-done, f32[1024,128]{1,0:T(8,128)S(1)} %bitcast.24, f32[2048,128]{1,0:T(8,128)} %param.10), kind=kLoop, calls=%fused_computation.6 | loop fusion | flops 1835008 | bytes 7340032 | tf_op jit(solution)/shard_map/concatenate | solution.py:31
  318.5 13.9 %gather_fusion.2 = f32[256,128,128]{2,1,0:T(8,128)} fusion(f32[56,128,128]{2,1,0:T(8,128)} %bitcast.22, s32[1024]{0:T(1024)S(1)} %pad_clamp_fusion), kind=kCustom, calls=%fused_computation.2 | custom fusion | bytes 33555456 | tf_op jit(solution)/shard_map/gather | solution.py:35
  332.5 21.2 %fusion = f32[16,128,128,1]{2,1,3,0:T(8,128)S(1)} fusion(f32[16,16,128,128]{3,2,1,0:T(8,128)} %bitcast.23, f32[16,16,128,128]{3,2,1,0:T(8,128)} %param.13, f32[16,16]{1,0:T(8,128)S(1)} %fusion.5), kind=kOutput, calls=%fused_computation.3 | convolution fusion | flops 6446645248 | bytes 34604032 | tf_op jit(solution)/shard_map/rtij,rtjh,rt->rih/dot_general | solution.py:36
  353.7 0.3 bitcast_divide_fusion
  354.1 1.2 multiply_reduce_fusion
  355.3 0.1 broadcast_multiply_fusion
  355.4 1.3 copy.13
  (7 shorter events, 0.0 us)
Async XLA Ops:
  6.5 347.5 %copy-start = (f32[128,128]{1,0:T(8,128)S(1)}, f32[128,128]{1,0:T(8,128)}, u32[]{:S(2)}) copy-start(f32[128,128]{1,0:T(8,128)} %param.18) | copy-start | bytes 196612
  6.5 308.1 %all-gather.3.cloned.1.call-start = ((), (), s32[]{:S(2)}) async-start(), calls=%async_computation.1 | async-start | bytes 2113536 | tf_op jit(solution)/shard_map/all_gather | solution.py:30
  15.8 25.7 %all-to-all-start = ((f32[128,8,128]{2,1,0:T(8,128)}), f32[128,8,128]{2,1,0:T(8,128)S(1)}, u32[]{:S(2)}, u32[]{:S(2)}) async-start(f32[128,8,128]{2,1,0:T(8,128)} %bitcast.1), calls=%async_computation | async-start | bytes 1048576 | tf_op jit(solution)/shard_map/all_to_all | solution.py:8
  332.5 21.6 %copy-start.1 = (f32[128]{0:T(128)S(1)}, f32[128]{0:T(128)}, u32[]{:S(2)}) copy-start(f32[128]{0:T(128)} %param.19) | copy-start | bytes 1540
Sparse Core Ops, SparseCore 0:
  9.8 304.8 all-gather.2
where the time goes:
time: 364 us
  waiting for transfers between devices  283 us (78%)
  matrix products  24.7 us (7%)
  local copies, waits for them, and re-layouts  23.2 us (6%)
  between operations  13.5 us (4%)
  starting transfers between devices  11.5 us (3%)
  other arithmetic  7.87 us (2%)
    all_gather x1, waiting for transfers between devices, body(): hub_table = lax.all_gather(own_hubs, ('dom', 'sub'), axis=0, tiled=True)  273 us
    dot_general x1, matrix products, body(): jnp.einsum('rtij,rtjh,rt->rih', tile_weights, blocks, slot_live, precisio...  21.2 us
    gather x1, local copies, waits for them, and re-layouts, body(): blocks = sources[tile_cols]  13.9 us
    all_to_all x1, starting transfers between devices, boundary_exchange(): lax.all_to_all(outgoing, ('dom', 'sub'), split_axis=0, concat_axis=0, til...  11.5 us
    all_to_all x1, waiting for transfers between devices, boundary_exchange(): lax.all_to_all(outgoing, ('dom', 'sub'), split_axis=0, concat_axis=0, til...  9.67 us
  transfers between devices with their start and end apart: 2, of which 2 were waited for; matrix products, arithmetic and copies ran while one was open for 3% of the time, Pallas kernels for 0%

commit v1 on v0

v1 whole, which is shorter than its diff:
```python
import functools

import jax
import jax.numpy as jnp
from jax import lax
from jax.experimental import pallas as pl
from jax.experimental.pallas import tpu as pltpu
from jax.sharding import PartitionSpec as P

MESH = pl.DeviceIdType.MESH
H = 128
NODE = 2048
ROW_TILES = 16
SLOTS = 16
DEVICES = 128
HUB = 32
BND = 8
HUB_AT = NODE + DEVICES * BND
SOURCES = HUB_AT + DEVICES * HUB


def steps(n):
    return 0 if n == 0 else (2 if n == 2 else 1)


def hub_tree():
    nodes = [(a, b, c) for a in range(4) for b in range(4) for c in range(4)]
    levels = [[n for n in nodes if sum(v != 0 for v in n) == k] for k in range(4)]
    load = {(d, s): 0.0 for d in range(3) for s in (1, 3)}
    parent = {}
    for level in levels[1:]:
        level.sort(key=lambda n: (sum(steps(v) for v in n), n))
        for n in level:
            best = None
            for d in range(3):
                if n[d] == 0:
                    continue
                uses = [(d, 1), (d, 3)] if n[d] == 2 else [(d, n[d])]
                key = (steps(n[d]), max(load[u] for u in uses), d)
                if best is None or key < best[0]:
                    best = (key, d, uses)
            _, d, uses = best
            for u in uses:
                load[u] += 1.0
            parent[n] = tuple(0 if i == d else v for i, v in enumerate(n))
    order = [n for level in levels for n in level]
    return levels, order, parent


LEVELS, ORDER, PARENT = hub_tree()
SLOT_OF = {n: i for i, n in enumerate(ORDER)}
CHILDREN = {n: [m for m in ORDER if PARENT.get(m) == n] for n in ORDER}
SWAPS = [(0, 1), (1, 9), (10, 27), (37, 27)]


def coords():
    dom = lax.axis_index("dom")
    sub = lax.axis_index("sub")
    z = lax.rem(lax.div(dom, 2), 2) * 2 + lax.div(sub, 4)
    return lax.div(dom, 4), lax.rem(sub, 4), z, lax.rem(dom, 2)


def device_at(x, y, z, c):
    return x * 4 + lax.div(z, 2) * 2 + c, lax.rem(z, 2) * 4 + y


def far_first(k):
    def offset(high, low):
        return jnp.where(high == 0, 2 - low, 3 * (1 - low))

    c = lax.rem(k, 2)
    h = lax.div(k, 16)
    low = lax.rem(lax.div(k, 2), 8)
    x = offset(lax.div(h, 4), lax.div(low, 4))
    y = offset(lax.rem(lax.div(h, 2), 2), lax.rem(lax.div(low, 2), 2))
    z = offset(lax.rem(h, 2), lax.rem(low, 2))
    return x, y, z, 1 - c


def split(v):
    hi = v.astype(jnp.bfloat16)
    lo = (v - hi.astype(jnp.float32)).astype(jnp.bfloat16)
    return hi, lo


def kernel(
    features,
    send_rows,
    hub_rows,
    weights,
    cols,
    count,
    degree,
    w_self,
    w_neigh,
    bias,
    out,
    feat,
    stage,
    parts,
    src,
    bnd_out,
    bnd,
    hub,
    hub_other,
    mean,
    base,
    feat_sem,
    stage_sem,
    hub_send,
    hub_recv,
    swap_send,
    swap_recv,
    bnd_send,
    bnd_recv,
):
    X, Y, Z, C = coords()

    def partner(x, y, z, c):
        return device_at(
            lax.rem(X + x, 4), lax.rem(Y + y, 4), lax.rem(Z + z, 4), lax.rem(C + c, 2)
        )

    barrier = pltpu.get_barrier_semaphore()

    def greet(k, _):
        pl.semaphore_signal(
            barrier, 1, device_id=partner(*far_first(k)), device_id_type=MESH
        )
        return 0

    lax.fori_loop(0, DEVICES - 1, greet, 0)

    feat_copy = pltpu.make_async_copy(features, feat, feat_sem)
    feat_copy.start()
    stage_copies = []
    for r in range(ROW_TILES):
        copy = pltpu.make_async_copy(weights.at[r], stage.at[r], stage_sem.at[r])
        copy.start()
        stage_copies.append(copy)

    feat_copy.wait()
    for i in range(HUB):
        hub[0, i] = feat[hub_rows[0, i]]
    pl.semaphore_wait(barrier, DEVICES - 1)

    def hub_copy(n):
        p = PARENT[n]
        move = tuple((a - b) % 4 for a, b in zip(n, p))
        return pltpu.make_async_remote_copy(
            src_ref=hub.at[SLOT_OF[p]],
            dst_ref=hub.at[SLOT_OF[n]],
            send_sem=hub_send,
            recv_sem=hub_recv.at[SLOT_OF[n]],
            device_id=partner(*move, 0),
            device_id_type=MESH,
        )

    def swap_copy(i):
        first, size = SWAPS[i]
        return pltpu.make_async_remote_copy(
            src_ref=hub.at[pl.ds(first, size)],
            dst_ref=hub_other.at[pl.ds(first, size)],
            send_sem=swap_send,
            recv_sem=swap_recv.at[i],
            device_id=partner(0, 0, 0, 1),
            device_id_type=MESH,
        )

    for n in CHILDREN[(0, 0, 0)]:
        hub_copy(n).start()
    swap_copy(0).start()

    me_dom = lax.axis_index("dom")
    me_sub = lax.axis_index("sub")
    me = me_dom * 8 + me_sub

    def gather(p, dst):
        for j in range(BND):
            dst[p, j] = feat[send_rows[j, p]]

    def send_boundary(k, _):
        dom, sub = partner(*far_first(k))
        p = dom * 8 + sub
        gather(p, bnd_out)
        pltpu.make_async_remote_copy(
            src_ref=bnd_out.at[p],
            dst_ref=bnd.at[me],
            send_sem=bnd_send,
            recv_sem=bnd_recv,
            device_id=(dom, sub),
            device_id_type=MESH,
        ).start()
        return 0

    lax.fori_loop(0, DEVICES - 1, send_boundary, 0)
    gather(me, bnd)

    def put(block, at, rows):
        hi, lo = split(rows)
        src[block, pl.ds(at, rows.shape[0]), 0:H] = hi
        src[block, pl.ds(at, rows.shape[0]), H:] = lo

    def put_features(i, _):
        at = pl.multiple_of(i * 128, 128)
        put(i, 0, feat[pl.ds(at, 128), :])
        return 0

    def convert(r):
        stage_copies[r].wait()
        deg = jnp.maximum(degree[r : r + 1, :], 1).astype(jnp.float32)
        scale = jnp.transpose(jnp.broadcast_to(1.0 / deg, (H, H)))

        def one(t, _):
            live = jnp.clip(count[r] - t, 0, 1).astype(jnp.float32)
            hi, lo = split(stage[r, t] * (scale * live))
            parts[r, t, 0:H, :] = hi
            parts[r, t, H:, :] = lo
            return 0

        lax.fori_loop(0, SLOTS, one, 0)

    def put_hub(table, core, level):
        for n in level:
            x, y, z = (lax.rem(v + 4 - o, 4) for v, o in zip((X, Y, Z), n))
            dom, sub = device_at(x, y, z, core)
            block = HUB_AT // 128 + dom * 2 + lax.div(sub, 4)
            at = pl.multiple_of(lax.rem(sub, 4) * HUB, HUB)
            put(block, at, table[SLOT_OF[n]])

    def arrive(level):
        for n in LEVELS[level]:
            hub_copy(n).wait_recv()
            for m in CHILDREN[n]:
                hub_copy(m).start()
        swap_copy(level).start()

    lax.fori_loop(0, ROW_TILES, put_features, 0)
    for r in range(0, 4):
        convert(r)
    arrive(1)
    put_hub(hub, C, LEVELS[0])
    put_hub(hub, C, LEVELS[1])
    for r in range(4, 8):
        convert(r)
    arrive(2)
    put_hub(hub, C, LEVELS[2])
    for r in range(8, 12):
        convert(r)
    ws_hi, ws_lo = split(w_self[...])
    both = jnp.concatenate([ws_hi, ws_hi], axis=0)

    def self_term(i, _):
        at = pl.multiple_of(i * 128, 128)
        rows = src[i]
        total = jnp.dot(rows, both, preferred_element_type=jnp.float32)
        total += jnp.dot(rows[:, 0:H], ws_lo, preferred_element_type=jnp.float32)
        base[pl.ds(at, 128), :] = total + bias[...]
        return 0

    lax.fori_loop(0, ROW_TILES, self_term, 0)
    for r in range(12, 16):
        convert(r)
    arrive(3)
    put_hub(hub, C, LEVELS[3])
    for i in range(4):
        swap_copy(i).wait_recv()
        put_hub(hub_other, 1 - C, LEVELS[i])
    others = pl.ds(0, DEVICES - 1)
    pltpu.make_async_copy(bnd_out.at[others], bnd.at[others], bnd_recv).wait()

    def put_boundary(i, _):
        rows = bnd[pl.ds(i * 16, 16)].reshape(128, H)
        put(NODE // 128 + i, 0, rows)
        return 0

    lax.fori_loop(0, DEVICES // 16, put_boundary, 0)

    def row_tile(r, _):
        lhs = jnp.concatenate([parts[r, t] for t in range(SLOTS)], axis=1)
        rhs = jnp.concatenate(
            [src[cols[r, t]] for t in range(SLOTS)], axis=0
        )
        res = jnp.dot(lhs, rhs, preferred_element_type=jnp.float32)
        total = (res[0:H, 0:H] + res[H:, H:]) + (res[0:H, H:] + res[H:, 0:H])
        mean[pl.ds(pl.multiple_of(r * 128, 128), 128), :] = total
        return 0

    lax.fori_loop(0, ROW_TILES, row_tile, 0)

    wn_hi, wn_lo = split(w_neigh[...])
    three = jnp.concatenate([wn_hi, wn_hi, wn_lo], axis=0)

    def finish(i, _):
        at = pl.multiple_of(i * 256, 256)
        hi, lo = split(mean[pl.ds(at, 256), :])
        rows = jnp.concatenate([hi, lo, hi], axis=1)
        hidden = base[pl.ds(at, 256), :] + jnp.dot(
            rows, three, preferred_element_type=jnp.float32
        )
        hidden = jnp.maximum(hidden, 0.0)
        square = jnp.mean(hidden * hidden, axis=-1, keepdims=True)
        out[pl.ds(at, 256), :] = hidden * lax.rsqrt(square + 1e-05)
        return 0

    lax.fori_loop(0, NODE // 256, finish, 0)

    tree = pl.ds(0, len(ORDER) - 1)
    pltpu.make_async_copy(hub.at[tree], hub.at[tree], hub_send).wait()
    pltpu.make_async_copy(hub, hub_other, swap_send).wait()
    pltpu.make_async_copy(bnd_out.at[others], bnd.at[others], bnd_send).wait()


def body(
    features,
    send_rows,
    hub_rows,
    tile_weights,
    tile_cols,
    tile_count,
    in_degree,
    w_self,
    w_neigh,
    bias,
):
    f32, bf16 = jnp.float32, jnp.bfloat16
    any_ = pl.BlockSpec(memory_space=pl.ANY)
    smem = pl.BlockSpec(memory_space=pltpu.SMEM)
    vmem = pl.BlockSpec(memory_space=pltpu.VMEM)
    dma = pltpu.SemaphoreType.DMA
    return pl.pallas_call(
        kernel,
        out_shape=jax.ShapeDtypeStruct((NODE, H), f32),
        in_specs=[any_, smem, smem, any_, smem, smem, vmem, vmem, vmem, vmem],
        out_specs=vmem,
        scratch_shapes=[
            pltpu.VMEM((NODE, H), f32),
            pltpu.VMEM((ROW_TILES, SLOTS, H, H), f32),
            pltpu.VMEM((ROW_TILES, SLOTS, 2 * H, H), bf16),
            pltpu.VMEM((SOURCES // 128, 128, 2 * H), bf16),
            pltpu.VMEM((DEVICES, BND, H), f32),
            pltpu.VMEM((DEVICES, BND, H), f32),
            pltpu.VMEM((64, HUB, H), f32),
            pltpu.VMEM((64, HUB, H), f32),
            pltpu.VMEM((NODE, H), f32),
            pltpu.VMEM((NODE, H), f32),
            dma,
            dma((ROW_TILES,)),
            dma,
            dma((64,)),
            dma,
            dma((4,)),
            dma,
            dma,
        ],
        compiler_params=pltpu.CompilerParams(
            collective_id=0, has_side_effects=True, vmem_limit_bytes=56 << 20
        ),
    )(
        features,
        jnp.swapaxes(send_rows, 1, 2).reshape(BND, DEVICES),
        hub_rows,
        tile_weights,
        tile_cols,
        tile_count,
        in_degree.reshape(ROW_TILES, H),
        w_self,
        w_neigh,
        bias.reshape(1, H),
    )


def solution(mesh):
    in_specs = (
        P(("dom", "sub"), None),
        P(("dom", "sub"), None, None),
        P(("dom", "sub"), None),
        P(("dom", "sub"), None, None, None),
        P(("dom", "sub"), None),
        P(("dom", "sub")),
        P(("dom", "sub")),
        P(),
        P(),
        P(),
    )
    out_specs = P(("dom", "sub"), None)
    return jax.shard_map(body, mesh=mesh, in_specs=in_specs, out_specs=out_specs, check_vma=False)
```

time: 364 us -> 52.4 us (0.14)
  waiting for transfers between devices: 283 us -> 0 us
  Pallas kernels: 0 us -> 49.9 us
  matrix products: 24.7 us -> 0 us
  local copies, waits for them, and re-layouts: 23.2 us -> 2.26 us
  between operations: 13.5 us -> 0.01 us
  starting transfers between devices: 11.5 us -> 0 us
  other arithmetic: 7.87 us -> 0 us
    all_gather x1 -> x0, waiting for transfers between devices: 273 us -> none  [body(): hub_table = lax.all_gather(own_hubs, ('dom', 'sub'), axis=0, tiled=True)]
    pallas_call x0 -> x1, Pallas kernels: none -> 49.9 us  [body(): pl.pallas_call(kernel, out_shape=jax.ShapeDtypeStruct((NODE, H), f32), in...]
    dot_general x3 -> x0, matrix products: 24.7 us -> none  [the longest x1 21.2 us: body(): jnp.einsum('rtij,rtjh,rt->rih', tile_weights, blocks, slot_live, precisio...]
    gather x3 -> x0, local copies, waits for them, and re-layouts: 21.6 us -> none  [the longest x1 13.9 us: body(): blocks = sources[tile_cols]]
    all_to_all x1 -> x0, starting transfers between devices: 11.5 us -> none  [boundary_exchange(): lax.all_to_all(outgoing, ('dom', 'sub'), split_axis=0, concat_axis=0, til...]
    all_to_all x1 -> x0, waiting for transfers between devices: 9.67 us -> none  [boundary_exchange(): lax.all_to_all(outgoing, ('dom', 'sub'), split_axis=0, concat_axis=0, til...]
    concatenate x1 -> x0, other arithmetic: 3.89 us -> none  [body(): jnp.concatenate([features, boundary, hub_table], axis=0)]
  transfers between devices with their start and end apart: 2 -> 0, of which waited for: 2 -> 0; matrix products, arithmetic and copies ran while one was open for 3% -> 0% of each run, Pallas kernels for 0% -> 0%
where the time goes in v1:
time: 52.4 us; the launch traced here: 52.2 us
  Pallas kernels  49.9 us (95%)
  local copies, waits for them, and re-layouts  2.26 us (4%)
    pallas_call x1, Pallas kernels, body(): pl.pallas_call(kernel, out_shape=jax.ShapeDtypeStruct((NODE, H), f32), in...  49.9 us
    unnamed x1, local copies, waits for them, and re-layouts  2.26 us

profile of v1, /device:TPU:1, one launch (start us, length us, event | category | flops | bytes accessed | tf_op | source)
XLA Modules:
  0.0 52.2 jit_solution(13779594872470796049)
XLA Ops:
  0.0 49.9 %shard_map.100 = f32[2048,128]{1,0:T(8,128)} custom-call(f32[2048,128]{1,0:T(8,128)} %features.1, s32[8,128]{1,0:T(8,128)} %bitcast.6, s32[1,32]{1,0:T(1,128)} %hub_rows.1, f32[16,16,128,128]{3,2,1,0:T(8,128)} %weights.1, s32[16,16]{1,0:T(8,128)} %cols.1, s32[16]{0:T(128)} %count.1, s32[16,128]{1,0:T(8,128)} %bitcast.5, f32[128,128]{1,0:T(8,128)} %w_self.1, ...), custom_call_target="tpu_custom_call" | custom-call | tf_op jit(solution)/shard_map/pallas_call | solution.py:331
  49.9 2.3 %copy.12 = f32[2048,128]{1,0:T(8,128)} copy(f32[2048,128]{1,0:T(8,128)} %shard_map.100) | data formatting | bytes 2097152

commit v2 on v1

v2 whole, which is shorter than its diff:
```python
import jax
import jax.numpy as jnp
from jax import lax
from jax.experimental import pallas as pl
from jax.experimental.pallas import tpu as pltpu
from jax.sharding import PartitionSpec as P

MESH = pl.DeviceIdType.MESH
H = 128
NODE = 2048
ROW_TILES = 16
SLOTS = 16
DEVICES = 128
HUB = 32
BND = 8
LOCAL_BLOCKS = NODE // 128
BND_BLOCKS = DEVICES * BND // 128
HUB_BLOCK = LOCAL_BLOCKS + BND_BLOCKS
BLOCKS = HUB_BLOCK + DEVICES * HUB // 128


def steps(n):
    return 0 if n == 0 else (2 if n == 2 else 1)


def distance(n):
    return sum(steps(v) for v in n)


def hub_tree():
    nodes = [(a, b, c) for a in range(4) for b in range(4) for c in range(4)]
    levels = [[n for n in nodes if sum(v != 0 for v in n) == k] for k in range(4)]
    load = {(d, s): 0.0 for d in range(3) for s in (1, 3)}
    parent = {}
    for level in levels[1:]:
        level.sort(key=lambda n: (distance(n), n))
        for n in level:
            best = None
            for d in range(3):
                if n[d] == 0:
                    continue
                uses = [(d, 1), (d, 3)] if n[d] == 2 else [(d, n[d])]
                key = (steps(n[d]), max(load[u] for u in uses), d)
                if best is None or key < best[0]:
                    best = (key, d, uses)
            _, d, uses = best
            for u in uses:
                load[u] += 1.0
            parent[n] = tuple(0 if i == d else v for i, v in enumerate(n))
    order = [n for level in levels for n in level]
    return levels, order, parent


LEVELS, ORDER, PARENT = hub_tree()
SLOT_OF = {n: i for i, n in enumerate(ORDER)}
CHILDREN = {n: [m for m in ORDER if PARENT.get(m) == n] for n in ORDER}
SWAPS = [(0, 1), (1, 9)] + [(10 + 9 * i, 9) for i in range(6)]
FAR_FIRST = sorted(
    ((x, y, z, c) for x in range(4) for y in range(4) for z in range(4) for c in range(2)),
    key=lambda n: (-distance(n[:3]), n),
)[:-2] + [(0, 0, 0, 1)]


def split(v):
    hi = v.astype(jnp.bfloat16)
    lo = (v - hi.astype(jnp.float32)).astype(jnp.bfloat16)
    return hi, lo


def kernel(
    features,
    send_rows_in,
    hub_rows_in,
    weights,
    cols_in,
    count_in,
    degree_in,
    w_self_in,
    w_neigh_in,
    bias_in,
    out,
    feat,
    send_rows,
    hub_rows,
    cols,
    count,
    degree,
    w_self,
    w_neigh,
    bias,
    stage,
    parts,
    src,
    bnd_out,
    bnd,
    hub,
    hub_other,
    base,
    small_sem,
    stage_sem,
    hub_send,
    hub_recv,
    swap_send,
    swap_recv,
    bnd_send,
    bnd_recv,
):
    dom = lax.axis_index("dom")
    sub = lax.axis_index("sub")
    me = dom * 8 + sub

    def partner(x, y, z, c=0):
        return dom ^ (x * 4 + (z // 2) * 2 + c), sub ^ ((z % 2) * 4 + y)

    barrier = pltpu.get_barrier_semaphore()
    for n in FAR_FIRST:
        pl.semaphore_signal(barrier, 1, device_id=partner(*n), device_id_type=MESH)

    fetched = []
    for i, (a, b) in enumerate(
        [
            (hub_rows_in, hub_rows),
            (features, feat),
            (send_rows_in, send_rows),
            (count_in, count),
            (degree_in, degree),
            (w_self_in, w_self),
            (w_neigh_in, w_neigh),
            (bias_in, bias),
            (cols_in, cols),
        ]
    ):
        copy = pltpu.make_async_copy(a, b, small_sem.at[i])
        copy.start()
        fetched.append(copy)
    stage_copies = []
    for r in range(ROW_TILES):
        copy = pltpu.make_async_copy(weights.at[r], stage.at[r], stage_sem.at[r])
        copy.start()
        stage_copies.append(copy)

    fetched[0].wait()
    fetched[1].wait()
    for i in range(HUB):
        hub[0, i] = feat[hub_rows[0, i]]
    pl.semaphore_wait(barrier, DEVICES - 1)

    def hub_copy(n):
        p = PARENT[n]
        return pltpu.make_async_remote_copy(
            src_ref=hub.at[SLOT_OF[p]],
            dst_ref=hub.at[SLOT_OF[n]],
            send_sem=hub_send,
            recv_sem=hub_recv.at[SLOT_OF[n]],
            device_id=partner(*(a ^ b for a, b in zip(n, p))),
            device_id_type=MESH,
        )

    def swap_copy(i):
        first, size = SWAPS[i]
        return pltpu.make_async_remote_copy(
            src_ref=hub.at[pl.ds(first, size)],
            dst_ref=hub_other.at[pl.ds(first, size)],
            send_sem=swap_send,
            recv_sem=swap_recv.at[i],
            device_id=partner(0, 0, 0, 1),
            device_id_type=MESH,
        )

    for n in CHILDREN[(0, 0, 0)]:
        hub_copy(n).start()
    swap_copy(0).start()

    fetched[2].wait()
    for n in FAR_FIRST:
        to = partner(*n)
        p = to[0] * 8 + to[1]
        for j in range(BND):
            bnd_out[p, j] = feat[send_rows[j, p]]
        pltpu.make_async_remote_copy(
            src_ref=bnd_out.at[p],
            dst_ref=bnd.at[me],
            send_sem=bnd_send,
            recv_sem=bnd_recv,
            device_id=to,
            device_id_type=MESH,
        ).start()
    for j in range(BND):
        bnd[me, j] = feat[send_rows[j, me]]

    def put(block, at, rows):
        hi, lo = split(rows)
        src[block, pl.ds(at, rows.shape[0]), 0:H] = hi
        src[block, pl.ds(at, rows.shape[0]), H:] = lo

    def put_features(i, _):
        put(i, 0, feat[pl.ds(pl.multiple_of(i * 128, 128), 128), :])
        return 0

    def convert(r):
        stage_copies[r].wait()
        deg = jnp.maximum(degree[r : r + 1, :], 1).astype(jnp.float32)
        scale = jnp.transpose(jnp.broadcast_to(1.0 / deg, (H, H)))

        def one(t, _):
            live = jnp.clip(count[r] - t, 0, 1).astype(jnp.float32)
            hi, lo = split(stage[r, t] * (scale * live))
            parts[r, t, 0:H, :] = hi
            parts[r, t, H:, :] = lo
            return 0

        lax.fori_loop(0, SLOTS, one, 0, unroll=4)

    def put_hub(table, core, nodes):
        for n in nodes:
            d, s = partner(*n)
            d = (d // 2) * 2 + core
            block = HUB_BLOCK + d * 2 + s // 4
            at = pl.multiple_of((s % 4) * HUB, HUB)
            put(block, at, table[SLOT_OF[n]])

    def arrive(level):
        for n in LEVELS[level]:
            hub_copy(n).wait_recv()
            for m in CHILDREN[n]:
                hub_copy(m).start()
            for i, (first, size) in enumerate(SWAPS):
                if SLOT_OF[n] == first + size - 1:
                    swap_copy(i).start()

    core = dom % 2
    fetched[3].wait()
    fetched[4].wait()
    for r in range(0, 3):
        convert(r)
    arrive(1)
    put_hub(hub, core, LEVELS[0] + LEVELS[1])
    for r in range(3, 8):
        convert(r)
    arrive(2)
    put_hub(hub, core, LEVELS[2])
    for r in range(8, 12):
        convert(r)
    lax.fori_loop(0, LOCAL_BLOCKS, put_features, 0)
    for copy in fetched[5:]:
        copy.wait()
    ws_hi, ws_lo = split(w_self[...])
    both = jnp.concatenate([ws_hi, ws_hi], axis=0)

    def self_term(i, _):
        rows = src[i]
        total = jnp.dot(rows, both, preferred_element_type=jnp.float32)
        total += jnp.dot(rows[:, 0:H], ws_lo, preferred_element_type=jnp.float32)
        base[pl.ds(pl.multiple_of(i * 128, 128), 128), :] = total + bias[...]
        return 0

    lax.fori_loop(0, ROW_TILES, self_term, 0, unroll=4)
    for r in range(12, 16):
        convert(r)
    arrive(3)
    put_hub(hub, core, LEVELS[3])
    for i, (first, size) in enumerate(SWAPS):
        swap_copy(i).wait_recv()
        put_hub(hub_other, 1 - core, ORDER[first : first + size])
    others = pl.ds(0, DEVICES - 1)
    pltpu.make_async_copy(bnd_out.at[others], bnd.at[others], bnd_recv).wait()

    def put_boundary(i, _):
        put(LOCAL_BLOCKS + i, 0, bnd[pl.ds(i * 16, 16)].reshape(128, H))
        return 0

    lax.fori_loop(0, BND_BLOCKS, put_boundary, 0)

    wn_hi, wn_lo = split(w_neigh[...])
    three = jnp.concatenate([wn_hi, wn_hi, wn_lo], axis=0)

    def row_tile(r):
        lhs = jnp.concatenate([parts[r, t] for t in range(SLOTS)], axis=1)
        rhs = jnp.concatenate([src[cols[r, t]] for t in range(SLOTS)], axis=0)
        res = jnp.dot(lhs, rhs, preferred_element_type=jnp.float32)
        return (res[0:H, 0:H] + res[H:, H:]) + (res[0:H, H:] + res[H:, 0:H])

    group = 4
    for g in range(0, ROW_TILES, group):
        rows = pl.ds(g * 128, group * 128)
        mean = jnp.concatenate([row_tile(g + i) for i in range(group)], axis=0)
        hi, lo = split(mean)
        hidden = base[rows, :] + jnp.dot(
            jnp.concatenate([hi, lo, hi], axis=1),
            three,
            preferred_element_type=jnp.float32,
        )
        hidden = jnp.maximum(hidden, 0.0)
        square = jnp.mean(hidden * hidden, axis=-1, keepdims=True)
        out[rows, :] = hidden * lax.rsqrt(square + 1e-05)

    tree = pl.ds(0, len(ORDER) - 1)
    pltpu.make_async_copy(hub.at[tree], hub.at[tree], hub_send).wait()
    pltpu.make_async_copy(hub, hub_other, swap_send).wait()
    pltpu.make_async_copy(bnd_out.at[others], bnd.at[others], bnd_send).wait()


def body(
    features,
    send_rows,
    hub_rows,
    tile_weights,
    tile_cols,
    tile_count,
    in_degree,
    w_self,
    w_neigh,
    bias,
):
    f32, bf16, i32 = jnp.float32, jnp.bfloat16, jnp.int32
    dma = pltpu.SemaphoreType.DMA
    vmem, smem = pltpu.VMEM, pltpu.SMEM
    return pl.pallas_call(
        kernel,
        out_shape=vmem((NODE, H), f32),
        in_specs=[pl.BlockSpec(memory_space=pl.ANY)] * 10,
        out_specs=pl.BlockSpec(memory_space=vmem),
        scratch_shapes=[
            vmem((NODE, H), f32),
            smem((BND, DEVICES), i32),
            smem((1, HUB), i32),
            smem((ROW_TILES, SLOTS), i32),
            smem((ROW_TILES,), i32),
            vmem((ROW_TILES, H), i32),
            vmem((H, H), f32),
            vmem((H, H), f32),
            vmem((1, H), f32),
            vmem((ROW_TILES, SLOTS, H, H), f32),
            vmem((ROW_TILES, SLOTS, 2 * H, H), bf16),
            vmem((BLOCKS, 128, 2 * H), bf16),
            vmem((DEVICES, BND, H), f32),
            vmem((DEVICES, BND, H), f32),
            vmem((64, HUB, H), f32),
            vmem((64, HUB, H), f32),
            vmem((NODE, H), f32),
            dma((9,)),
            dma((ROW_TILES,)),
            dma,
            dma((64,)),
            dma,
            dma((len(SWAPS),)),
            dma,
            dma,
        ],
        compiler_params=pltpu.CompilerParams(
            collective_id=0, has_side_effects=True, vmem_limit_bytes=56 << 20
        ),
    )(
        features,
        jnp.swapaxes(send_rows, 1, 2).reshape(BND, DEVICES),
        hub_rows,
        tile_weights,
        tile_cols,
        tile_count,
        in_degree.reshape(ROW_TILES, H),
        w_self,
        w_neigh,
        bias.reshape(1, H),
    )


def solution(mesh):
    in_specs = (
        P(("dom", "sub"), None),
        P(("dom", "sub"), None, None),
        P(("dom", "sub"), None),
        P(("dom", "sub"), None, None, None),
        P(("dom", "sub"), None),
        P(("dom", "sub")),
        P(("dom", "sub")),
        P(),
        P(),
        P(),
    )
    out_specs = P(("dom", "sub"), None)
    return jax.shard_map(body, mesh=mesh, in_specs=in_specs, out_specs=out_specs, check_vma=False)
```

time: 52.4 us -> 36.2 us (0.69)
  Pallas kernels: 49.9 us -> 35.1 us
  local copies, waits for them, and re-layouts: 2.26 us -> 0.97 us
    pallas_call x1, Pallas kernels: 49.9 us -> 35.1 us  [body(): pl.pallas_call(kernel, out_shape=vmem((NODE, H), f32), in_specs=[pl.Block...]
    unnamed x1, local copies, waits for them, and re-layouts: 2.26 us -> 0.97 us
where the time goes in v2:
time: 36.2 us; the launch traced here: 36.1 us
  Pallas kernels  35.1 us (97%)
  local copies, waits for them, and re-layouts  0.97 us (3%)
    pallas_call x1, Pallas kernels, body(): pl.pallas_call(kernel, out_shape=vmem((NODE, H), f32), in_specs=[pl.Block...  35.1 us
    unnamed x1, local copies, waits for them, and re-layouts  0.97 us

profile of v2, /device:TPU:1, one launch (start us, length us, event | category | flops | bytes accessed | tf_op | source)
XLA Modules:
  0.0 36.1 jit_solution(3114448064276772059)
XLA Ops:
  0.0 35.1 %shard_map.100 = f32[2048,128]{1,0:T(8,128)S(1)} custom-call(f32[2048,128]{1,0:T(8,128)} %features.1, s32[8,128]{1,0:T(8,128)} %bitcast.6, s32[1,32]{1,0:T(1,128)} %hub_rows_in.1, f32[16,16,128,128]{3,2,1,0:T(8,128)} %weights.1, s32[16,16]{1,0:T(8,128)} %cols_in.1, s32[16]{0:T(128)} %count_in.1, s32[16,128]{1,0:T(8,128)} %bitcast.5, f32[128,128]{1,0:T(8,128)} %w_self_in.1, ...), custom_call_target="tpu_custom_call" | custom-call | tf_op jit(solution)/shard_map/pallas_call | solution.py:318
  35.1 1.0 %copy.12 = f32[2048,128]{1,0:T(8,128)} copy(f32[2048,128]{1,0:T(8,128)S(1)} %shard_map.100) | data formatting | bytes 2097152

commit v3 on v2

--- a/solution.py
+++ b/solution.py
@@ -55,10 +55,71 @@
 SLOT_OF = {n: i for i, n in enumerate(ORDER)}
 CHILDREN = {n: [m for m in ORDER if PARENT.get(m) == n] for n in ORDER}
 SWAPS = [(0, 1), (1, 9)] + [(10 + 9 * i, 9) for i in range(6)]
+def link_uses(n):
+    uses = []
+    for d, v in enumerate(n[:3]):
+        uses += [(d, 1)] * (v in (1, 2)) + [(d, 3)] * (v in (2, 3))
+    return uses
+
+
+def spread_out(nodes):
+    load = {(d, s): 0.0 for d in range(3) for s in (1, 3)}
+    left, result = list(nodes), []
+    while left:
+
+        def cost(n):
+            uses = link_uses(n)
+            return (load[uses[0]] * 3 + sum(load[u] for u in uses[1:])) / len(uses), n
+
+        best = min(left, key=cost)
+        left.remove(best)
+        result.append(best)
+        for u in load:
+            load[u] *= 0.7
+        for u in link_uses(best):
+            load[u] += 1.0
+    return result
+
+
+def link_uses(n):
+    uses = []
+    for d, v in enumerate(n[:3]):
+        uses += [(d, 1)] * (v in (1, 2)) + [(d, 3)] * (v in (2, 3))
+    return uses
+
+
+def spread_out(nodes):
+    load = {(d, s): 0.0 for d in range(3) for s in (1, 3)}
+    left, result = list(nodes), []
+    while left:
+
+        def cost(n):
+            uses = link_uses(n)
+            return (load[uses[0]] * 3 + sum(load[u] for u in uses[1:])) / len(uses), n
+
+        best = min(left, key=cost)
+        left.remove(best)
+        result.append(best)
+        for u in load:
+            load[u] *= 0.7
+        for u in link_uses(best):
+            load[u] += 1.0
+    return result
+
+
 FAR_FIRST = sorted(
     ((x, y, z, c) for x in range(4) for y in range(4) for z in range(4) for c in range(2)),
     key=lambda n: (-distance(n[:3]), n),
 )[:-2] + [(0, 0, 0, 1)]
+
+
+def both_cores(nodes):
+    first = [n + (i % 2,) for i, n in enumerate(nodes)]
+    return first + [(x, y, z, 1 - c) for x, y, z, c in first]
+
+
+EXCHANGE = [both_cores(spread_out(level)) for level in LEVELS[1:]]
+EXCHANGE[0].append((0, 0, 0, 1))
 
 
 def split(v):
@@ -102,6 +163,8 @@
     hub_recv,
     swap_send,
     swap_recv,
+    plane_sem,
+    cube_sem,
     bnd_send,
     bnd_recv,
 ):
@@ -113,7 +176,7 @@
         return dom ^ (x * 4 + (z // 2) * 2 + c), sub ^ ((z % 2) * 4 + y)
 
     barrier = pltpu.get_barrier_semaphore()
-    for n in FAR_FIRST:
+    for n in EXCHANGE[0]:
         pl.semaphore_signal(barrier, 1, device_id=partner(*n), device_id_type=MESH)
 
     fetched = []
@@ -136,14 +199,17 @@
     stage_copies = []
     for r in range(ROW_TILES):
         copy = pltpu.make_async_copy(weights.at[r], stage.at[r], stage_sem.at[r])
-        copy.start()
         stage_copies.append(copy)
 
     fetched[0].wait()
     fetched[1].wait()
     for i in range(HUB):
         hub[0, i] = feat[hub_rows[0, i]]
-    pl.semaphore_wait(barrier, DEVICES - 1)
+    pl.semaphore_wait(barrier, len(EXCHANGE[0]))
+
+    def tell(sem):
+        for n in LEVELS[1]:
+            pl.semaphore_signal(sem, 1, device_id=partner(*n), device_id_type=MESH)
 
     def hub_copy(n):
         p = PARENT[n]
@@ -170,9 +236,11 @@
     for n in CHILDREN[(0, 0, 0)]:
         hub_copy(n).start()
     swap_copy(0).start()
+    tell(plane_sem)
 
     fetched[2].wait()
-    for n in FAR_FIRST:
+    def send_boundary(nodes):
+      for n in nodes:
         to = partner(*n)
         p = to[0] * 8 + to[1]
         for j in range(BND):
@@ -185,6 +253,8 @@
             device_id=to,
             device_id_type=MESH,
         ).start()
+    send_boundary(EXCHANGE[0])
+    for c in stage_copies: c.start()
     for j in range(BND):
         bnd[me, j] = feat[send_rows[j, me]]
 
@@ -231,13 +301,19 @@
     core = dom % 2
     fetched[3].wait()
     fetched[4].wait()
+    pl.semaphore_wait(plane_sem, len(LEVELS[1]))
+    tell(cube_sem)
+    send_boundary(EXCHANGE[1])
     for r in range(0, 3):
         convert(r)
     arrive(1)
+    pl.semaphore_wait(cube_sem, len(LEVELS[1]))
+    send_boundary(EXCHANGE[2][:27])
     put_hub(hub, core, LEVELS[0] + LEVELS[1])
     for r in range(3, 8):
         convert(r)
     arrive(2)
+    send_boundary(EXCHANGE[2][27:])
     put_hub(hub, core, LEVELS[2])
     for r in range(8, 12):
         convert(r)
@@ -344,6 +420,8 @@
             dma((64,)),
             dma,
             dma((len(SWAPS),)),
+            pltpu.SemaphoreType.REGULAR,
+            pltpu.SemaphoreType.REGULAR,
             dma,
             dma,
         ],

time: 36.2 us -> 30.6 us (0.85)
  Pallas kernels: 35.1 us -> 29.5 us
    pallas_call x1, Pallas kernels: 35.1 us -> 29.5 us  [body(): pl.pallas_call(kernel, out_shape=vmem((NODE, H), f32), in_specs=[pl.Block...]
where the time goes in v3:
time: 30.6 us; the launch traced here: 30.5 us
  Pallas kernels  29.5 us (96%)
  local copies, waits for them, and re-layouts  0.97 us (3%)
    pallas_call x1, Pallas kernels, body(): pl.pallas_call(kernel, out_shape=vmem((NODE, H), f32), in_specs=[pl.Block...  29.5 us
    unnamed x1, local copies, waits for them, and re-layouts  0.97 us

profile of v3, /device:TPU:1, one launch (start us, length us, event | category | flops | bytes accessed | tf_op | source)
XLA Modules:
  0.0 30.5 jit_solution(17367163327469257438)
XLA Ops:
  0.0 29.5 %shard_map.100 = f32[2048,128]{1,0:T(8,128)S(1)} custom-call(f32[2048,128]{1,0:T(8,128)} %features.1, s32[8,128]{1,0:T(8,128)} %bitcast.6, s32[1,32]{1,0:T(1,128)} %hub_rows_in.1, f32[16,16,128,128]{3,2,1,0:T(8,128)} %weights.1, s32[16,16]{1,0:T(8,128)} %cols_in.1, s32[16]{0:T(128)} %count_in.1, s32[16,128]{1,0:T(8,128)} %bitcast.5, f32[128,128]{1,0:T(8,128)} %w_self_in.1, ...), custom_call_target="tpu_custom_call" | custom-call | tf_op jit(solution)/shard_map/pallas_call | solution.py:394
  29.5 1.0 %copy.12 = f32[2048,128]{1,0:T(8,128)} copy(f32[2048,128]{1,0:T(8,128)S(1)} %shard_map.100) | data formatting | bytes 2097152

commit v4 on v3

--- a/solution.py
+++ b/solution.py
@@ -201,10 +201,6 @@
         copy = pltpu.make_async_copy(weights.at[r], stage.at[r], stage_sem.at[r])
         stage_copies.append(copy)
 
-    fetched[0].wait()
-    fetched[1].wait()
-    for i in range(HUB):
-        hub[0, i] = feat[hub_rows[0, i]]
     pl.semaphore_wait(barrier, len(EXCHANGE[0]))
 
     def tell(sem):
@@ -233,10 +229,14 @@
             device_id_type=MESH,
         )
 
+    tell(plane_sem)
+    fetched[0].wait()
+    fetched[1].wait()
+    for i in range(HUB):
+        hub[0, i] = feat[hub_rows[0, i]]
     for n in CHILDREN[(0, 0, 0)]:
         hub_copy(n).start()
     swap_copy(0).start()
-    tell(plane_sem)
 
     fetched[2].wait()
     def send_boundary(nodes):
@@ -323,6 +323,9 @@
     ws_hi, ws_lo = split(w_self[...])
     both = jnp.concatenate([ws_hi, ws_hi], axis=0)
 
+    wn_hi, wn_lo = split(w_neigh[...])
+    three = jnp.concatenate([wn_hi, wn_hi, wn_lo], axis=0)
+
     def self_term(i, _):
         rows = src[i]
         total = jnp.dot(rows, both, preferred_element_type=jnp.float32)
@@ -345,10 +348,7 @@
         put(LOCAL_BLOCKS + i, 0, bnd[pl.ds(i * 16, 16)].reshape(128, H))
         return 0
 
-    lax.fori_loop(0, BND_BLOCKS, put_boundary, 0)
-
-    wn_hi, wn_lo = split(w_neigh[...])
-    three = jnp.concatenate([wn_hi, wn_hi, wn_lo], axis=0)
+    lax.fori_loop(0, BND_BLOCKS, put_boundary, 0, unroll=True)
 
     def row_tile(r):
         lhs = jnp.concatenate([parts[r, t] for t in range(SLOTS)], axis=1)
@@ -356,7 +356,7 @@
         res = jnp.dot(lhs, rhs, preferred_element_type=jnp.float32)
         return (res[0:H, 0:H] + res[H:, H:]) + (res[0:H, H:] + res[H:, 0:H])
 
-    group = 4
+    group = 8
     for g in range(0, ROW_TILES, group):
         rows = pl.ds(g * 128, group * 128)
         mean = jnp.concatenate([row_tile(g + i) for i in range(group)], axis=0)

time: 30.6 us -> 30.3 us (level)
  no operation moved by 1% of the time
where the time goes in v4:
time: 30.3 us; the launch traced here: 30.2 us
  Pallas kernels  29.2 us (96%)
  local copies, waits for them, and re-layouts  0.97 us (3%)
    pallas_call x1, Pallas kernels, body(): pl.pallas_call(kernel, out_shape=vmem((NODE, H), f32), in_specs=[pl.Block...  29.2 us
    unnamed x1, local copies, waits for them, and re-layouts  0.97 us

profile of v4, /device:TPU:1, one launch (start us, length us, event | category | flops | bytes accessed | tf_op | source)
XLA Modules:
  0.0 30.2 jit_solution(12886970432760298525)
XLA Ops:
  0.0 29.2 %shard_map.100 = f32[2048,128]{1,0:T(8,128)S(1)} custom-call(f32[2048,128]{1,0:T(8,128)} %features.1, s32[8,128]{1,0:T(8,128)} %bitcast.6, s32[1,32]{1,0:T(1,128)} %hub_rows_in.1, f32[16,16,128,128]{3,2,1,0:T(8,128)} %weights.1, s32[16,16]{1,0:T(8,128)} %cols_in.1, s32[16]{0:T(128)} %count_in.1, s32[16,128]{1,0:T(8,128)} %bitcast.5, f32[128,128]{1,0:T(8,128)} %w_self_in.1, ...), custom_call_target="tpu_custom_call" | custom-call | tf_op jit(solution)/shard_map/pallas_call | solution.py:394
  29.2 1.0 %copy.12 = f32[2048,128]{1,0:T(8,128)} copy(f32[2048,128]{1,0:T(8,128)S(1)} %shard_map.100) | data formatting | bytes 2097152
